TPU v7x, 128 devices: a whole 4x4x4 slice. The times are simulated.
128 devices in a mesh: narrow: 8 (over z_lo, x), wide: 16 (over z_hi, y, core).
Axes of the slice: x: 4, y: 4, z: 4 (z_hi: 2, z_lo: 2; z = z_hi * 2 + z_lo), core: 2. Of those that a mesh axis runs over, the one named last changes fastest.
Arguments:
- source: float32 [262144, 128], P(('narrow', 'wide')), may hold values from -6 to 6
- interp_maps: float32 [18, 2, 2, 128, 128], replicated, may hold values from -0.375 to 0.375
- phases: float32 [18, 262144, 64], P(None, ('narrow', 'wide')), may hold values from -3.140625 to 3.140625
Outputs:
- targets: float32 [262144, 128], P(('narrow', 'wide'))
All inputs are finite; a program needn't handle non-finite values.
Results may differ from a plain program's by a relative error of at most 0.0003.
Values sent between devices are 32-bit elements; how exact they have to be, the bound alone decides.
No kernel may reach another device: no remote copies, remote signals or barrier semaphores. Data moves between devices by JAX's collectives and lax.ppermute only.
A program may use at most 128 MiB of HBM per device.

v0:
```python
import functools

import jax
import jax.numpy as jnp
from jax import lax
from jax.experimental import pallas as pl
from jax.experimental.pallas import tpu as pltpu
from jax.sharding import PartitionSpec as P

AXES = ("narrow", "wide")
SIN_HALF = (0.9999999957157406, -0.041666644924359314, 0.0005208156633383668, -3.095163447075199e-06, 1.0176428087056766e-08)
COS_HALF = (0.9999999532465265, -0.12499976265264102, 0.002603973680502671, -2.1646354078657635e-05, 9.044205735375736e-08)
CHUNK = 256
VMEM = 58 * 2**20


def horner(coefficients, z):
    total = jnp.full_like(z, coefficients[-1])
    for c in coefficients[-2::-1]:
        total = total * z + c
    return total


def cos_sin(x):
    z = x * x
    s = x * horner(SIN_HALF, z)
    c = horner(COS_HALF, z)
    return 1.0 - 0.5 * (s * s), s * c


def spread(cosine, sine, parity):
    left = lax.broadcasted_iota(jnp.int32, cosine.shape, 1) < 64
    c_roll = pltpu.roll(cosine, 64, 1)
    s_roll = pltpu.roll(sine, 64, 1)
    if parity == 0:
        return jnp.where(left, cosine, c_roll), jnp.where(left, -sine, s_roll)
    return jnp.where(left, c_roll, cosine), jnp.where(left, -s_roll, sine)


def rotate(values, cosine, sine, parity):
    c2, s2 = spread(cosine, sine, parity)
    return values * c2 + pltpu.roll(values, 64, 1) * s2


def dot3(x, w):
    upper = x.astype(jnp.bfloat16)
    lower = (x - upper.astype(jnp.float32)).astype(jnp.bfloat16)
    w = jnp.concatenate([w[: x.shape[1]], w], axis=0)
    return jnp.dot(jnp.concatenate([upper, lower, upper], axis=1), w, preferred_element_type=jnp.float32)


def row_slices(stride, step, n=CHUNK):
    if stride >= n:
        per = stride // n
        return [pl.ds((step // per) * 2 * stride + (step % per) * n, n)]
    base = step * 2 * n
    if stride >= 8:
        return [pl.ds(base + j * 2 * stride, stride) for j in range(n // stride)]
    return [pl.ds(base + o, n // stride, stride=2 * stride) for o in range(stride)]


def shifted(s, by):
    return pl.ds(s.start + by, s.size, stride=s.stride)


def load_pairs(ref, slices, stride):
    def cat(parts):
        return parts[0] if len(parts) == 1 else jnp.concatenate(parts, axis=0)

    return cat([ref[s, :] for s in slices]), cat([ref[shifted(s, stride), :] for s in slices])


def store_pairs(ref, slices, stride, low, high):
    at = 0
    for s in slices:
        ref[s, :] = low[at : at + s.size]
        ref[shifted(s, stride), :] = high[at : at + s.size]
        at += s.size


def pair_level(state, cosine, sine, w, stride, parity, put=None, ready=None):
    rows = state.shape[0]

    for i in range(rows // (2 * CHUNK)):
        if ready is not None:
            ready(i)
        slices = row_slices(stride, i)
        low, high = load_pairs(state, slices, stride)
        new = dot3(jnp.concatenate([low, high], axis=1), w)
        c_low, c_high = load_pairs(cosine, slices, stride)
        s_low, s_high = load_pairs(sine, slices, stride)
        low = rotate(new[:, :128], c_low, s_low, parity)
        high = rotate(new[:, 128:], c_high, s_high, parity)
        if put is None:
            store_pairs(state, slices, stride, low, high)
        else:
            put(i, low, high)


def pack_kernel(first, parts, phases, out, angles, packed, come, gone):
    levels, _, columns = angles.shape
    size = columns // parts
    devices = size // 16

    def arrive(i):
        at = pl.ds(i * size, size)
        return pltpu.make_async_copy(phases.at[pl.ds(first, levels), :, at], angles.at[:, :, at], come.at[i])

    def leave(i):
        at = pl.ds(i * devices, devices)
        return pltpu.make_async_copy(packed.at[at], out.at[at], gone.at[i])

    for i in range(parts):
        arrive(i).start()
    for i in range(parts):
        arrive(i).wait()
        for j in range(i * size // 128, (i + 1) * size // 128):
            for k in range(levels // 2):
                at = pl.ds(j * 128, 128)
                block = jnp.concatenate([angles[2 * k, :, at], angles[2 * k + 1, :, at]], axis=0)
                packed[pl.ds(j * 8, 8), pl.ds(k * 16, 16), :] = block.T.reshape(8, 16, 128)
        leave(i).start()
    for i in range(parts):
        leave(i).wait()


def halves(w):
    upper = w.astype(jnp.bfloat16)
    return jnp.concatenate([upper, (w - upper.astype(jnp.float32)).astype(jnp.bfloat16)], axis=0)


def split_map(maps):
    return halves(jnp.concatenate([jnp.concatenate([maps[0, i], maps[1, i]], axis=1) for i in range(2)], axis=0))


def split_map_planes(maps):
    real, imag = slice(0, 64), slice(64, 128)
    return halves(
        jnp.concatenate(
            [jnp.concatenate([maps[o, i][:, part] for part in (real, imag) for o in range(2)], axis=1) for i in range(2)], axis=0
        )
    )


def local_kernel(levels, source, phases, maps, state, cosine, sine):
    pair = pl.program_id(0)

    @pl.when(pair == 0)
    def _():
        state[...] = source[...]

    def angles(j, carry):
        at = pl.ds(pl.multiple_of(j * 128, 128), 128)
        block = jnp.concatenate([phases[0, :, at], phases[1, :, at]], axis=0)
        c, s = cos_sin(block.T)
        cosine[at, :] = c
        sine[at, :] = s
        return carry

    lax.fori_loop(0, phases.shape[2] // 128, angles, 0, unroll=4)
    for level in range(levels):

        @pl.when(pair == level // 2)
        def _():
            pair_level(state, cosine, sine, split_map(maps[level % 2]), 2**level, level % 2)


def core_kernel(parity_ref, own, partner, cosine, sine, maps, out):
    odd = parity_ref[0] == 1
    w = halves(jnp.concatenate([maps[0, 0, 0], maps[0, 0, 1]], axis=0))

    def step(i, carry):
        at = pl.ds(pl.multiple_of(i * CHUNK, CHUNK), CHUNK)
        mine, other = own[at, :], partner[at, :]
        low = jnp.where(odd, other, mine)
        high = jnp.where(odd, mine, other)
        new = dot3(jnp.concatenate([low, high], axis=1), w)
        out[at, :] = rotate(new, cosine[at, :], sine[at, :], 1)
        return carry

    lax.fori_loop(0, own.shape[0] // CHUNK, step, 0)


def angles_kernel(boxes, angles, maps, waves, weights, cos_rows, sin_rows):
    rows = cos_rows.shape[0]
    level = 2 * pl.program_id(0)
    c, s = cos_sin(angles[...].reshape(rows, 128))
    cos_rows[...] = c
    sin_rows[...] = s
    left = lax.broadcasted_iota(jnp.int32, (CHUNK, 128), 1) < 64
    for pair in range(3):

        @pl.when(pl.program_id(0) == pair)
        def _():
            for parity in range(2):
                stride = boxes * 2 ** (2 * pair + parity + 1)
                for i in range(rows // (2 * CHUNK)):
                    for which, here in enumerate((cos_rows, sin_rows)):
                        low, high = load_pairs(here, row_slices(stride, i), stride)
                        if parity == 0:
                            both = jnp.where(left, low, pltpu.roll(high, 64, 1))
                        else:
                            both = jnp.where(left, pltpu.roll(low, 64, 1), high)
                        waves[parity, which, pl.ds(i * CHUNK, CHUNK), :] = both

    for parity in range(2):
        weights[parity] = split_map_planes(maps[parity])


def plane_level(state, waves, w, stride, put=None):
    left = lax.broadcasted_iota(jnp.int32, (CHUNK, 128), 1) < 64
    for i in range(state.shape[0] // (2 * CHUNK)):
        slices = row_slices(stride, i)
        low, high = load_pairs(state, slices, stride)
        new = dot3(jnp.concatenate([low, high], axis=1), w)
        at = pl.ds(i * CHUNK, CHUNK)
        c, s = waves[0, at, :], waves[1, at, :]
        real, imag = new[:, :128], new[:, 128:]
        real, imag = real * c - imag * s, real * s + imag * c
        low = jnp.where(left, real, pltpu.roll(imag, 64, 1))
        high = jnp.where(left, pltpu.roll(real, 64, 1), imag)
        if put is None:
            store_pairs(state, slices, stride, low, high)
        else:
            put(i, low, high)


def final_kernel(levels, boxes, source, waves, weights, out, state, waves_here, w_here, turned, come, gone):
    steps = state.shape[0] // (2 * CHUNK)
    n = CHUNK // boxes
    half = out.shape[1] // 2

    def arrive(level):
        here = [
            pltpu.make_async_copy(weights.at[level], w_here.at[level], come.at[3 * level]),
            pltpu.make_async_copy(waves.at[level], waves_here.at[level], come.at[3 * level + 1]),
        ]
        return ([pltpu.make_async_copy(source, state, come.at[2])] if level == 0 else []) + here

    def leave(i, upper):
        at = pl.ds(upper * half + i * n, n)
        return pltpu.make_async_copy(turned.at[:, at, :], out.at[:, at, :], gone.at[2 * i + upper])

    def put(i, low, high):
        for upper, values in enumerate((low, high)):
            turned[:, pl.ds(upper * half + i * n, n), :] = jnp.swapaxes(values.reshape(n, boxes, 128), 0, 1)
            leave(i, upper).start()

    for level in range(levels):
        for copy in arrive(level):
            copy.start()
    groups = (0, 1, 3, 6)
    for level in range(levels):
        if level in groups:
            for other in range(level, groups[groups.index(level) + 1]):
                for copy in arrive(other):
                    copy.wait()
        plane_level(state, waves_here.at[level], w_here[level], boxes * 2 ** (level + 1), put if level == levels - 1 else None)
    for i in range(steps):
        leave(i, 0).wait()
        leave(i, 1).wait()


def params():
    return pltpu.CompilerParams(vmem_limit_bytes=VMEM)


def cost(microseconds, moved):
    return pl.CostEstimate(flops=int(microseconds * 1e9), bytes_accessed=moved, transcendentals=0)


def per_device(source, interp_maps, phases):
    box_dev, columns = source.shape
    f32 = jnp.float32
    devices = lax.axis_size("narrow") * lax.axis_size("wide")
    per_peer = box_dev // devices
    local = box_dev.bit_length() - 1
    levels = interp_maps.shape[0]
    first = local + 1
    pairs = (levels - first) // 2
    turned = jnp.transpose(phases, (0, 2, 1))
    points = turned.shape[1]

    parts = 4
    packed = pl.pallas_call(
        functools.partial(pack_kernel, first, parts),
        in_specs=[pl.BlockSpec(memory_space=pl.ANY)],
        out_specs=pl.BlockSpec(memory_space=pl.ANY),
        out_shape=jax.ShapeDtypeStruct((devices, pairs * per_peer, columns), f32),
        scratch_shapes=[
            pltpu.VMEM((2 * pairs, points, box_dev), f32),
            pltpu.VMEM((devices, pairs * per_peer, columns), f32),
            pltpu.SemaphoreType.DMA((parts,)),
            pltpu.SemaphoreType.DMA((parts,)),
        ],
        compiler_params=params(),
        cost_estimate=cost(2, 6 << 20),
        name="pack_phases",
    )(turned)
    arrived = lax.all_to_all(packed, AXES, split_axis=0, concat_axis=0, tiled=True)

    whole = jax.ShapeDtypeStruct((box_dev, columns), f32)
    whole_spec = pl.BlockSpec((box_dev, columns), lambda k: (0, 0))
    state, cosine, sine = pl.pallas_call(
        functools.partial(local_kernel, local),
        grid=(first // 2,),
        in_specs=[
            whole_spec,
            pl.BlockSpec((2, points, box_dev), lambda k: (k, 0, 0)),
            pl.BlockSpec((2, 2, 2, columns, columns), lambda k: (k, 0, 0, 0, 0)),
        ],
        out_specs=[whole_spec] * 3,
        out_shape=[whole] * 3,
        compiler_params=params(),
        cost_estimate=cost(20, 18 << 20),
        name="local_levels",
    )(source, turned, interp_maps)

    wide = lax.axis_size("wide")
    partner = lax.ppermute(state, "wide", [(i, i ^ 1) for i in range(wide)])
    parity = jnp.reshape(lax.axis_index("wide") & 1, (1,)).astype(jnp.int32)
    state = pl.pallas_call(
        core_kernel,
        grid_spec=pltpu.PrefetchScalarGridSpec(
            num_scalar_prefetch=1,
            grid=(4,),
            in_specs=[pl.BlockSpec((box_dev // 4, columns), lambda k, p: (k, 0))] * 4
            + [pl.BlockSpec((1, 1, 2, columns, columns), lambda k, p: (first - 1, p[0], 0, 0, 0))],
            out_specs=pl.BlockSpec((box_dev // 4, columns), lambda k, p: (k, 0)),
        ),
        out_shape=whole,
        compiler_params=params(),
        cost_estimate=cost(3, 5 << 20),
        name="core_level",
    )(parity, state, partner, cosine, sine, interp_maps)

    state, arrived = lax.optimization_barrier((state, arrived))
    state = lax.all_to_all(state.reshape(devices, per_peer, columns), AXES, split_axis=0, concat_axis=0, tiled=True)

    waves_shape = (2 * pairs, 2, box_dev // 2, columns)
    waves, weights = pl.pallas_call(
        functools.partial(angles_kernel, per_peer),
        grid=(pairs,),
        in_specs=[
            pl.BlockSpec((devices, per_peer, columns), lambda k: (0, k, 0)),
            pl.BlockSpec((2, 2, 2, columns, columns), lambda k: (first // 2 + k, 0, 0, 0, 0)),
        ],
        out_specs=[
            pl.BlockSpec((2, *waves_shape[1:]), lambda k: (k, 0, 0, 0)),
            pl.BlockSpec((2, 4 * columns, 2 * columns), lambda k: (k, 0, 0)),
        ],
        out_shape=[jax.ShapeDtypeStruct(waves_shape, f32), jax.ShapeDtypeStruct((2 * pairs, 4 * columns, 2 * columns), jnp.bfloat16)],
        scratch_shapes=[pltpu.VMEM((box_dev, columns), f32)] * 2,
        compiler_params=params(),
        cost_estimate=cost(6, 9 << 20),
        name="angles",
    )(arrived, interp_maps)

    steps = box_dev // (2 * CHUNK)
    out = pl.pallas_call(
        functools.partial(final_kernel, levels - first, per_peer),
        in_specs=[pl.BlockSpec(memory_space=pl.ANY)] * 3,
        out_specs=pl.BlockSpec(memory_space=pl.ANY),
        out_shape=jax.ShapeDtypeStruct((per_peer, devices, columns), f32),
        scratch_shapes=[
            pltpu.VMEM((box_dev, columns), f32),
            pltpu.VMEM(waves_shape, f32),
            pltpu.VMEM((2 * pairs, 4 * columns, 2 * columns), jnp.bfloat16),
            pltpu.VMEM((per_peer, devices, columns), f32),
            pltpu.SemaphoreType.DMA((6 * pairs,)),
            pltpu.SemaphoreType.DMA((2 * steps,)),
        ],
        compiler_params=params(),
        cost_estimate=cost(6, 10 << 20),
        name="final_levels",
    )(state.reshape(box_dev, columns), waves, weights)
    return out.reshape(box_dev, columns)


def solution(mesh):
    in_specs = (P(AXES, None), P(), P(None, AXES, None))
    return jax.shard_map(per_device, mesh=mesh, in_specs=in_specs, out_specs=P(AXES, None), check_vma=False)
```

profile of v0, /device:TPU:1, one launch (start us, length us, event | category | flops | bytes accessed | tf_op | source)
XLA Modules:
  0.0 89.6 jit_solution(11390559037048955343)
XLA Ops:
  0.0 3.2 %pack_phases.1 = f32[128,48,128]{2,1,0:T(8,128)} custom-call(f32[18,64,2048]{2,1,0:T(8,128)} %bitcast.5), custom_call_target="tpu_custom_call" | custom-call | flops 2000000000 | bytes 6291456 | tf_op jit(solution)/shard_map/pack_phases/pallas_call | solution.py:285
  3.2 11.5 %all-to-all-start = ((f32[128,48,128]{2,1,0:T(8,128)}), f32[128,48,128]{2,1,0:T(8,128)S(1)}, u32[]{:S(2)}, u32[]{:S(2)}) async-start(f32[128,48,128]{2,1,0:T(8,128)} %pack_phases.1), calls=%async_computation | async-start | bytes 6291456 | tf_op jit(solution)/shard_map/all_to_all | solution.py:300
  14.7 21.0 %local_levels.1 = (f32[2048,128]{1,0:T(8,128)}, f32[2048,128]{1,0:T(8,128)}, f32[2048,128]{1,0:T(8,128)}) custom-call(f32[2048,128]{1,0:T(8,128)} %source.1, f32[18,64,2048]{2,1,0:T(8,128)} %bitcast.6, f32[18,2,2,128,128]{4,3,2,1,0:T(8,128)} %maps.5), custom_call_target="tpu_custom_call" | custom-call | flops 20000000000 | bytes 18874368 | tf_op jit(solution)/shard_map/local_levels/pallas_call | solution.py:304
  35.7 1.1 %collective-permute-start = (f32[2048,128]{1,0:T(8,128)}, f32[2048,128]{1,0:T(8,128)}, u32[]{:S(2)}, u32[]{:S(2)}) collective-permute-start(f32[2048,128]{1,0:T(8,128)} %get-tuple-element.12.own), channel_id=1, source_target_pairs={{0,1},{1,0},{2,3},{3,2},{4,5},{5,4},{6,7},{7,6},{8,9},{9,8},{10,11... | collective-permute-start | bytes 3145736 | tf_op jit(solution)/shard_map/ppermute | solution.py:320
  36.8 2.6 %collective-permute-done.partner = f32[2048,128]{1,0:T(8,128)} collective-permute-done((f32[2048,128]{1,0:T(8,128)}, f32[2048,128]{1,0:T(8,128)}, u32[]{:S(2)}, u32[]{:S(2)}) %collective-permute-start) | collective-permute-done | bytes 1048608 | tf_op jit(solution)/shard_map/ppermute | solution.py:320
  39.4 5.4 %core_level.1 = f32[2048,128]{1,0:T(8,128)} custom-call(s32[1]{0:T(128)} %bitcast.parity_ref, f32[2048,128]{1,0:T(8,128)} %get-tuple-element.12.own, f32[2048,128]{1,0:T(8,128)} %collective-permute-done.partner, f32[2048,128]{1,0:T(8,128)} %get-tuple-element.13.cosine, f32[2048,128]{1,0:T(8,128)} %get-tuple-element.14.sine, f32[18,2,2,128,128]{4,3,2,1,0:T(8,128)} %maps.5), custom_call_target="tpu_custom_call" | custom-call | flops 3000000000 | bytes 5242880 | tf_op jit(solution)/shard_map/core_level/pallas_call | solution.py:322
  44.8 14.3 %all-to-all-done.angles = f32[128,48,128]{2,1,0:T(8,128)S(1)} async-done(((f32[128,48,128]{2,1,0:T(8,128)}), f32[128,48,128]{2,1,0:T(8,128)S(1)}, u32[]{:S(2)}, u32[]{:S(2)}) %all-to-all-start) | async-done | bytes 3145760 | tf_op jit(solution)/shard_map/all_to_all | solution.py:300
  59.1 0.0 copy-start
  59.1 5.2 %all-to-all-start.1 = ((f32[128,16,128]{2,1,0:T(8,128)}), f32[128,16,128]{2,1,0:T(8,128)}, u32[]{:S(2)}, u32[]{:S(2)}) async-start(f32[128,16,128]{2,1,0:T(8,128)} %bitcast.7), calls=%async_computation.1 | async-start | bytes 2097152 | tf_op jit(solution)/shard_map/all_to_all | solution.py:338
  64.4 0.0 copy-done
  64.4 8.1 %angles.1 = (f32[6,2,1024,128]{3,2,1,0:T(8,128)}, bf16[6,512,256]{2,1,0:T(8,128)(2,1)}) custom-call(f32[128,48,128]{2,1,0:T(8,128)} %copy-done, f32[18,2,2,128,128]{4,3,2,1,0:T(8,128)} %maps.5), custom_call_target="tpu_custom_call" | custom-call | flops 6000000000 | bytes 9437184 | tf_op jit(solution)/shard_map/angles/pallas_call | solution.py:341
  72.5 10.5 %all-to-all-done.1 = f32[128,16,128]{2,1,0:T(8,128)} async-done(((f32[128,16,128]{2,1,0:T(8,128)}), f32[128,16,128]{2,1,0:T(8,128)}, u32[]{:S(2)}, u32[]{:S(2)}) %all-to-all-start.1) | async-done | bytes 1048608 | tf_op jit(solution)/shard_map/all_to_all | solution.py:338
  82.9 6.5 %final_levels.1 = f32[16,128,128]{2,1,0:T(8,128)} custom-call(f32[2048,128]{1,0:T(8,128)} %bitcast.3.source, f32[6,2,1024,128]{3,2,1,0:T(8,128)} %get-tuple-element.17.waves, bf16[6,512,256]{2,1,0:T(8,128)(2,1)} %get-tuple-element.18.weights), custom_call_target="tpu_custom_call" | custom-call | flops 6000000000 | bytes 10485760 | tf_op jit(solution)/shard_map/final_levels/pallas_call | solution.py:360
Async XLA Ops:
  3.2 55.9 %all-to-all-start = ((f32[128,48,128]{2,1,0:T(8,128)}), f32[128,48,128]{2,1,0:T(8,128)S(1)}, u32[]{:S(2)}, u32[]{:S(2)}) async-start(f32[128,48,128]{2,1,0:T(8,128)} %pack_phases.1), calls=%async_computation | async-start | bytes 6291456 | tf_op jit(solution)/shard_map/all_to_all | solution.py:300
  35.7 3.7 %collective-permute-start = (f32[2048,128]{1,0:T(8,128)}, f32[2048,128]{1,0:T(8,128)}, u32[]{:S(2)}, u32[]{:S(2)}) collective-permute-start(f32[2048,128]{1,0:T(8,128)} %get-tuple-element.12.own), channel_id=1, source_target_pairs={{0,1},{1,0},{2,3},{3,2},{4,5},{5,4},{6,7},{7,6},{8,9},{9,8},{10,11... | collective-permute-start | bytes 3145736 | tf_op jit(solution)/shard_map/ppermute | solution.py:320
  59.1 5.3 %copy-start = (f32[128,48,128]{2,1,0:T(8,128)}, f32[128,48,128]{2,1,0:T(8,128)S(1)}, u32[]{:S(2)}) copy-start(f32[128,48,128]{2,1,0:T(8,128)S(1)} %all-to-all-done.angles) | copy-start | bytes 9437188
  59.1 23.8 %all-to-all-start.1 = ((f32[128,16,128]{2,1,0:T(8,128)}), f32[128,16,128]{2,1,0:T(8,128)}, u32[]{:S(2)}, u32[]{:S(2)}) async-start(f32[128,16,128]{2,1,0:T(8,128)} %bitcast.7), calls=%async_computation.1 | async-start | bytes 2097152 | tf_op jit(solution)/shard_map/all_to_all | solution.py:338
where the time goes:
time: 90 us; the launch traced here: 89.6 us
  Pallas kernels  44.2 us (49%)
  waiting for transfers between devices  27.4 us (30%)
  starting transfers between devices  17.8 us (20%)
    pallas_call x1, Pallas kernels, per_device(): pl.pallas_call(functools.partial(local_kernel, local), grid=(first // 2,)...  21 us
    all_to_all x1, waiting for transfers between devices, per_device(): lax.all_to_all(packed, AXES, split_axis=0, concat_axis=0, tiled=True)  14.3 us
    all_to_all x1, starting transfers between devices, per_device(): lax.all_to_all(packed, AXES, split_axis=0, concat_axis=0, tiled=True)  11.5 us
    all_to_all x1, waiting for transfers between devices, per_device(): lax.all_to_all(state.reshape(devices, per_peer, columns), AXES, split_axi...  10.5 us
    pallas_call x1, Pallas kernels, per_device(): pl.pallas_call(functools.partial(angles_kernel, per_peer), grid=(pairs,),...  8.1 us
    pallas_call x1, Pallas kernels, per_device(): pl.pallas_call(functools.partial(final_kernel, levels - first, per_peer),...  6.47 us
    pallas_call x1, Pallas kernels, per_device(): pl.pallas_call(core_kernel, grid_spec=pltpu.PrefetchScalarGridSpec(num_sc...  5.42 us
    all_to_all x1, starting transfers between devices, per_device(): lax.all_to_all(state.reshape(devices, per_peer, columns), AXES, split_axi...  5.24 us
  transfers between devices with their start and end apart: 3, of which 3 were waited for; matrix products, arithmetic and copies ran while one was open for 0% of the time, Pallas kernels for 39%

commit v1 on v0

--- a/solution.py
+++ b/solution.py
@@ -157,7 +157,7 @@
         sine[at, :] = s
         return carry
 
-    lax.fori_loop(0, phases.shape[2] // 128, angles, 0, unroll=4)
+    lax.fori_loop(0, phases.shape[2] // 128, angles, 0, unroll=True)
     for level in range(levels):
 
         @pl.when(pair == level // 2)

time: 90 us -> 90 us (level)
  Pallas kernels: 44.2 us -> 42.8 us
  waiting for transfers between devices: 27.4 us -> 28.8 us
    all_to_all x1, waiting for transfers between devices: 14.3 us -> 15.7 us  [per_device(): lax.all_to_all(packed, AXES, split_axis=0, concat_axis=0, tiled=True)]
    pallas_call x1, Pallas kernels: 21 us -> 19.6 us  [per_device(): pl.pallas_call(functools.partial(local_kernel, local), grid=(first // 2,)...]
  transfers between devices with their start and end apart: 3 -> 3, of which waited for: 3 -> 3; matrix products, arithmetic and copies ran while one was open for 0% -> 0% of each run, Pallas kernels for 39% -> 37%
where the time goes in v1:
time: 90 us; the launch traced here: 89.6 us
  Pallas kernels  42.8 us (48%)
  waiting for transfers between devices  28.8 us (32%)
  starting transfers between devices  17.8 us (20%)
    pallas_call x1, Pallas kernels, per_device(): pl.pallas_call(functools.partial(local_kernel, local), grid=(first // 2,)...  19.6 us
    all_to_all x1, waiting for transfers between devices, per_device(): lax.all_to_all(packed, AXES, split_axis=0, concat_axis=0, tiled=True)  15.7 us
    all_to_all x1, starting transfers between devices, per_device(): lax.all_to_all(packed, AXES, split_axis=0, concat_axis=0, tiled=True)  11.5 us
    all_to_all x1, waiting for transfers between devices, per_device(): lax.all_to_all(state.reshape(devices, per_peer, columns), AXES, split_axi...  10.5 us
    pallas_call x1, Pallas kernels, per_device(): pl.pallas_call(functools.partial(angles_kernel, per_peer), grid=(pairs,),...  8.1 us
    pallas_call x1, Pallas kernels, per_device(): pl.pallas_call(functools.partial(final_kernel, levels - first, per_peer),...  6.47 us
    pallas_call x1, Pallas kernels, per_device(): pl.pallas_call(core_kernel, grid_spec=pltpu.PrefetchScalarGridSpec(num_sc...  5.42 us
    all_to_all x1, starting transfers between devices, per_device(): lax.all_to_all(state.reshape(devices, per_peer, columns), AXES, split_axi...  5.24 us
  transfers between devices with their start and end apart: 3, of which 3 were waited for; matrix products, arithmetic and copies ran while one was open for 0% of the time, Pallas kernels for 37%

profile of v1, /device:TPU:1, one launch (start us, length us, event | category | flops | bytes accessed | tf_op | source)
XLA Modules:
  0.0 89.6 jit_solution(5780308962967169788)
XLA Ops:
  0.0 3.2 %pack_phases.1 = f32[128,48,128]{2,1,0:T(8,128)} custom-call(f32[18,64,2048]{2,1,0:T(8,128)} %bitcast.5), custom_call_target="tpu_custom_call" | custom-call | flops 2000000000 | bytes 6291456 | tf_op jit(solution)/shard_map/pack_phases/pallas_call | solution.py:285
  3.2 11.5 %all-to-all-start = ((f32[128,48,128]{2,1,0:T(8,128)}), f32[128,48,128]{2,1,0:T(8,128)S(1)}, u32[]{:S(2)}, u32[]{:S(2)}) async-start(f32[128,48,128]{2,1,0:T(8,128)} %pack_phases.1), calls=%async_computation | async-start | bytes 6291456 | tf_op jit(solution)/shard_map/all_to_all | solution.py:300
  14.7 19.6 %local_levels.1 = (f32[2048,128]{1,0:T(8,128)}, f32[2048,128]{1,0:T(8,128)}, f32[2048,128]{1,0:T(8,128)}) custom-call(f32[2048,128]{1,0:T(8,128)} %source.1, f32[18,64,2048]{2,1,0:T(8,128)} %bitcast.6, f32[18,2,2,128,128]{4,3,2,1,0:T(8,128)} %maps.5), custom_call_target="tpu_custom_call" | custom-call | flops 20000000000 | bytes 18874368 | tf_op jit(solution)/shard_map/local_levels/pallas_call | solution.py:304
  34.3 1.0 %collective-permute-start = (f32[2048,128]{1,0:T(8,128)}, f32[2048,128]{1,0:T(8,128)}, u32[]{:S(2)}, u32[]{:S(2)}) collective-permute-start(f32[2048,128]{1,0:T(8,128)} %get-tuple-element.12.own), channel_id=1, source_target_pairs={{0,1},{1,0},{2,3},{3,2},{4,5},{5,4},{6,7},{7,6},{8,9},{9,8},{10,11... | collective-permute-start | bytes 3145736 | tf_op jit(solution)/shard_map/ppermute | solution.py:320
  35.3 2.6 %collective-permute-done.partner = f32[2048,128]{1,0:T(8,128)} collective-permute-done((f32[2048,128]{1,0:T(8,128)}, f32[2048,128]{1,0:T(8,128)}, u32[]{:S(2)}, u32[]{:S(2)}) %collective-permute-start) | collective-permute-done | bytes 1048608 | tf_op jit(solution)/shard_map/ppermute | solution.py:320
  38.0 5.4 %core_level.1 = f32[2048,128]{1,0:T(8,128)} custom-call(s32[1]{0:T(128)} %bitcast.parity_ref, f32[2048,128]{1,0:T(8,128)} %get-tuple-element.12.own, f32[2048,128]{1,0:T(8,128)} %collective-permute-done.partner, f32[2048,128]{1,0:T(8,128)} %get-tuple-element.13.cosine, f32[2048,128]{1,0:T(8,128)} %get-tuple-element.14.sine, f32[18,2,2,128,128]{4,3,2,1,0:T(8,128)} %maps.5), custom_call_target="tpu_custom_call" | custom-call | flops 3000000000 | bytes 5242880 | tf_op jit(solution)/shard_map/core_level/pallas_call | solution.py:322
  43.4 15.7 %all-to-all-done.angles = f32[128,48,128]{2,1,0:T(8,128)S(1)} async-done(((f32[128,48,128]{2,1,0:T(8,128)}), f32[128,48,128]{2,1,0:T(8,128)S(1)}, u32[]{:S(2)}, u32[]{:S(2)}) %all-to-all-start) | async-done | bytes 3145760 | tf_op jit(solution)/shard_map/all_to_all | solution.py:300
  59.1 0.0 copy-start
  59.1 5.2 %all-to-all-start.1 = ((f32[128,16,128]{2,1,0:T(8,128)}), f32[128,16,128]{2,1,0:T(8,128)}, u32[]{:S(2)}, u32[]{:S(2)}) async-start(f32[128,16,128]{2,1,0:T(8,128)} %bitcast.7), calls=%async_computation.1 | async-start | bytes 2097152 | tf_op jit(solution)/shard_map/all_to_all | solution.py:338
  64.4 0.0 copy-done
  64.4 8.1 %angles.1 = (f32[6,2,1024,128]{3,2,1,0:T(8,128)}, bf16[6,512,256]{2,1,0:T(8,128)(2,1)}) custom-call(f32[128,48,128]{2,1,0:T(8,128)} %copy-done, f32[18,2,2,128,128]{4,3,2,1,0:T(8,128)} %maps.5), custom_call_target="tpu_custom_call" | custom-call | flops 6000000000 | bytes 9437184 | tf_op jit(solution)/shard_map/angles/pallas_call | solution.py:341
  72.5 10.5 %all-to-all-done.1 = f32[128,16,128]{2,1,0:T(8,128)} async-done(((f32[128,16,128]{2,1,0:T(8,128)}), f32[128,16,128]{2,1,0:T(8,128)}, u32[]{:S(2)}, u32[]{:S(2)}) %all-to-all-start.1) | async-done | bytes 1048608 | tf_op jit(solution)/shard_map/all_to_all | solution.py:338
  82.9 6.5 %final_levels.1 = f32[16,128,128]{2,1,0:T(8,128)} custom-call(f32[2048,128]{1,0:T(8,128)} %bitcast.3.source, f32[6,2,1024,128]{3,2,1,0:T(8,128)} %get-tuple-element.17.waves, bf16[6,512,256]{2,1,0:T(8,128)(2,1)} %get-tuple-element.18.weights), custom_call_target="tpu_custom_call" | custom-call | flops 6000000000 | bytes 10485760 | tf_op jit(solution)/shard_map/final_levels/pallas_call | solution.py:360
Async XLA Ops:
  3.2 55.9 %all-to-all-start = ((f32[128,48,128]{2,1,0:T(8,128)}), f32[128,48,128]{2,1,0:T(8,128)S(1)}, u32[]{:S(2)}, u32[]{:S(2)}) async-start(f32[128,48,128]{2,1,0:T(8,128)} %pack_phases.1), calls=%async_computation | async-start | bytes 6291456 | tf_op jit(solution)/shard_map/all_to_all | solution.py:300
  34.3 3.7 %collective-permute-start = (f32[2048,128]{1,0:T(8,128)}, f32[2048,128]{1,0:T(8,128)}, u32[]{:S(2)}, u32[]{:S(2)}) collective-permute-start(f32[2048,128]{1,0:T(8,128)} %get-tuple-element.12.own), channel_id=1, source_target_pairs={{0,1},{1,0},{2,3},{3,2},{4,5},{5,4},{6,7},{7,6},{8,9},{9,8},{10,11... | collective-permute-start | bytes 3145736 | tf_op jit(solution)/shard_map/ppermute | solution.py:320
  59.1 5.3 %copy-start = (f32[128,48,128]{2,1,0:T(8,128)}, f32[128,48,128]{2,1,0:T(8,128)S(1)}, u32[]{:S(2)}) copy-start(f32[128,48,128]{2,1,0:T(8,128)S(1)} %all-to-all-done.angles) | copy-start | bytes 9437188
  59.1 23.8 %all-to-all-start.1 = ((f32[128,16,128]{2,1,0:T(8,128)}), f32[128,16,128]{2,1,0:T(8,128)}, u32[]{:S(2)}, u32[]{:S(2)}) async-start(f32[128,16,128]{2,1,0:T(8,128)} %bitcast.7), calls=%async_computation.1 | async-start | bytes 2097152 | tf_op jit(solution)/shard_map/all_to_all | solution.py:338
